TPU v7x, 256 devices: a whole 4x4x8 slice. The times are simulated.
256 devices in a mesh: seq: 32 (over z, y_lo, core), head: 8 (over x, y_hi).
Axes of the slice: x: 4, y: 4 (y_hi: 2, y_lo: 2; y = y_hi * 2 + y_lo), z: 8, core: 2. Of those that a mesh axis runs over, the one named last changes fastest.
Arguments:
- queries: bfloat16 [2048, 8192], P('seq', 'head'), may hold values from -15 to 15
- cache_keys: bfloat16 [8, 32768, 128], P('head', 'seq'), may hold values from -6 to 6
- cache_values: bfloat16 [8, 32768, 128], P('head', 'seq'), may hold values from -6 to 6
- new_keys: bfloat16 [2048, 1024], P('seq', 'head'), may hold values from -9.5625 to 9.5625
- new_values: bfloat16 [2048, 1024], P('seq', 'head'), may hold values from -6 to 6
- cache_len: int32 [32], P('seq'), may hold values from 256 to 1024, as said below
- span_rank: int32 [2048], replicated, may hold values from 0 to 2047, each once
- out_weight: bfloat16 [8192, 8192], P('head', 'seq'), may hold values from -0.0625 to 0.0625
Outputs:
- projected: bfloat16 [2048, 8192], P('head', 'seq')
Inputs may be any that keep to these rules, and one draw needn't show every extreme that they name: `cache_len`: each shard holds at least 256 filled positions; one shard is full in every draw.
All inputs are finite; a program needn't handle non-finite values.
Results may differ from a plain program's by a relative error of at most 0.006.
Values may be sent and summed in bfloat16 or wider, within the bound.
No kernel may reach another device: no remote copies, remote signals or barrier semaphores. Data moves between devices by JAX's collectives and lax.ppermute only.
A program may use at most 64 MiB of HBM per device.

v0:
```python
import math

import jax
import jax.numpy as jnp
from jax import lax
from jax.sharding import PartitionSpec as P

BLOCK = 512


NEG_FILL = -1e30


def shifted(value, axis, steps):
    count = lax.axis_size(axis)
    pairs = [(source, (source + steps) % count) for source in range(count)]
    return lax.ppermute(value, axis, pairs)


def combine(earlier, latter):
    sum_a, max_a, tot_a = earlier
    sum_b, max_b, tot_b = latter
    overall = jnp.maximum(max_a, max_b)
    factor_a = jnp.exp(max_a - overall)
    factor_b = jnp.exp(max_b - overall)
    return (
        sum_a * factor_a[..., None] + sum_b * factor_b[..., None],
        overall,
        tot_a * factor_a + tot_b * factor_b,
    )


def block_terms(query_rows, key_rows, value_rows, usable, score_scale):
    scores = jnp.dot(query_rows, key_rows.T, preferred_element_type=jnp.float32) * score_scale
    scores = jnp.where(usable, scores, NEG_FILL)
    row_max = jnp.max(scores, axis=1)
    weights = jnp.where(usable, jnp.exp(scores - row_max[:, None]), 0.0).astype(jnp.bfloat16)
    row_sum = jnp.sum(weights.astype(jnp.float32), axis=1)
    summed = jnp.dot(weights, value_rows, preferred_element_type=jnp.float32)
    return (summed, row_max, row_sum)


def shard_terms(
    query_rows, query_rank, key_rows, value_rows, length, new_key_rows, new_value_rows, own_rank
):
    head_dim = key_rows.shape[1]
    score_scale = jnp.float32(1.0 / math.sqrt(head_dim))
    row_total = query_rows.shape[0]

    def visit(block_at, running):
        offset = block_at * BLOCK
        key_block = lax.dynamic_slice_in_dim(key_rows, offset, BLOCK, 0)
        value_block = lax.dynamic_slice_in_dim(value_rows, offset, BLOCK, 0)
        usable = offset + jnp.arange(BLOCK, dtype=jnp.int32) < length
        usable = jnp.broadcast_to(usable[None, :], (row_total, BLOCK))
        return combine(
            running, block_terms(query_rows, key_block, value_block, usable, score_scale)
        )

    initial = (
        jnp.zeros((row_total, head_dim), jnp.float32),
        jnp.full((row_total,), NEG_FILL, jnp.float32),
        jnp.zeros((row_total,), jnp.float32),
    )
    blocks = (length + BLOCK - 1) // BLOCK
    running = lax.fori_loop(0, blocks, visit, initial)
    usable_new = own_rank[None, :] <= query_rank[:, None]
    return combine(
        running, block_terms(query_rows, new_key_rows, new_value_rows, usable_new, score_scale)
    )


def body(queries, cache_keys, cache_values, new_keys, new_values, cache_len, span_rank, out_weight):
    tokens = queries.shape[0]
    head_dim = cache_keys.shape[2]
    head_count = queries.shape[1] // head_dim
    key_rows = cache_keys[0]
    value_rows = cache_values[0]
    length = cache_len[0]
    my_index = lax.axis_index("seq")
    shard_count = lax.axis_size("seq")
    own_rank = lax.dynamic_slice_in_dim(span_rank, my_index * tokens, tokens)

    def local(query_rows, query_rank):
        return shard_terms(
            query_rows, query_rank, key_rows, value_rows, length, new_keys, new_values, own_rank
        )

    def anchor_rank(anchor, width):
        return jnp.repeat(lax.dynamic_slice_in_dim(span_rank, anchor * tokens, tokens), width)

    def cycle_step(step_no, state):
        travelling, running = state
        anchor = (my_index - step_no) % shard_count
        part = local(
            travelling.reshape(tokens * head_count, head_dim), anchor_rank(anchor, head_count)
        )
        running = combine(running, part)
        travelling = shifted(travelling, "seq", 1)
        running = shifted((running[0], running[1], running[2]), "seq", 1)
        return (travelling, running)

    rows_here = tokens * head_count
    final_state = lax.fori_loop(
        0,
        shard_count,
        cycle_step,
        (
            queries,
            (
                jnp.zeros((rows_here, head_dim), jnp.float32),
                jnp.full((rows_here,), NEG_FILL, jnp.float32),
                jnp.zeros((rows_here,), jnp.float32),
            ),
        ),
    )
    running = final_state[1]
    attended = (
        (running[0] / running[2][:, None])
        .astype(jnp.bfloat16)
        .reshape(tokens, head_count * head_dim)
    )
    attended_every = lax.all_gather(attended, "seq", axis=0, tiled=True)
    projected = lax.psum_scatter(
        jnp.dot(attended_every, out_weight, preferred_element_type=jnp.float32),
        "head",
        scatter_dimension=0,
        tiled=True,
    )
    return projected.astype(jnp.bfloat16)


def solution(mesh):
    return jax.shard_map(
        body,
        mesh=mesh,
        in_specs=(
            P("seq", "head"),
            P("head", "seq", None),
            P("head", "seq", None),
            P("seq", "head"),
            P("seq", "head"),
            P("seq"),
            P(),
            P("head", "seq"),
        ),
        out_specs=P("head", "seq"),
        check_vma=False,
    )
```

profile of v0, /device:TPU:1, one launch (start us, length us, event | category | flops | bytes accessed | tf_op | source)
XLA Modules:
  0.0 769.0 jit_solution(13603516997068444564)
XLA Ops:
  9.0 592.2 %while.77 = (s32[]{:T(128)}, bf16[64,1024]{1,0:T(8,128)(2,1)S(1)}, f32[512,128]{1,0:T(8,128)S(1)}, f32[512]{0:T(512)S(1)}, f32[512]{0:T(512)S(1)}, /*index=5*/s3...) while((s32[]{:T(128)}, bf16[64,1024]{1,0:T(8,128)(2,1)S(1)}, ...), condition=%wide.region_7.8_spmd, body=%wide.region_0.7_spmd.sunk | while | flops 154935296 | bytes 8003999 | solution.py:104
  10.1 7.3 while.78
  26.8 7.3 while.78
  43.3 7.3 while.78
  61.8 7.3 while.78
  80.5 7.3 while.78
  99.1 7.3 while.78
  117.7 7.3 while.78
  127.5 7.8 %collective-permute-done.2 = f32[512]{0:T(512)S(1)} collective-permute-done((f32[512]{0:T(512)S(1)}, f32[512]{0:T(512)S(1)}, u32[]{:S(2)}, u32[]{:S(2)}) %collective-permute-start.2) | collective-permute-done | bytes 2080 | tf_op jit(solution)/shard_map/while/body/eval_jaxpr/ppermute | solution.py:17
  136.4 7.3 while.78
  144.9 9.0 %collective-permute-done.2 = f32[512]{0:T(512)S(1)} collective-permute-done((f32[512]{0:T(512)S(1)}, f32[512]{0:T(512)S(1)}, u32[]{:S(2)}, u32[]{:S(2)}) %collective-permute-start.2) | collective-permute-done | bytes 2080 | tf_op jit(solution)/shard_map/while/body/eval_jaxpr/ppermute | solution.py:17
  155.0 7.3 while.78
  163.5 9.0 %collective-permute-done.2 = f32[512]{0:T(512)S(1)} collective-permute-done((f32[512]{0:T(512)S(1)}, f32[512]{0:T(512)S(1)}, u32[]{:S(2)}, u32[]{:S(2)}) %collective-permute-start.2) | collective-permute-done | bytes 2080 | tf_op jit(solution)/shard_map/while/body/eval_jaxpr/ppermute | solution.py:17
  173.7 7.3 while.78
  182.1 9.0 %collective-permute-done.2 = f32[512]{0:T(512)S(1)} collective-permute-done((f32[512]{0:T(512)S(1)}, f32[512]{0:T(512)S(1)}, u32[]{:S(2)}, u32[]{:S(2)}) %collective-permute-start.2) | collective-permute-done | bytes 2080 | tf_op jit(solution)/shard_map/while/body/eval_jaxpr/ppermute | solution.py:17
  192.3 7.3 while.78
  200.7 9.0 %collective-permute-done.2 = f32[512]{0:T(512)S(1)} collective-permute-done((f32[512]{0:T(512)S(1)}, f32[512]{0:T(512)S(1)}, u32[]{:S(2)}, u32[]{:S(2)}) %collective-permute-start.2) | collective-permute-done | bytes 2080 | tf_op jit(solution)/shard_map/while/body/eval_jaxpr/ppermute | solution.py:17
  210.9 7.3 while.78
  219.4 9.0 %collective-permute-done.2 = f32[512]{0:T(512)S(1)} collective-permute-done((f32[512]{0:T(512)S(1)}, f32[512]{0:T(512)S(1)}, u32[]{:S(2)}, u32[]{:S(2)}) %collective-permute-start.2) | collective-permute-done | bytes 2080 | tf_op jit(solution)/shard_map/while/body/eval_jaxpr/ppermute | solution.py:17
  229.6 7.3 while.78
  238.0 9.0 %collective-permute-done.2 = f32[512]{0:T(512)S(1)} collective-permute-done((f32[512]{0:T(512)S(1)}, f32[512]{0:T(512)S(1)}, u32[]{:S(2)}, u32[]{:S(2)}) %collective-permute-start.2) | collective-permute-done | bytes 2080 | tf_op jit(solution)/shard_map/while/body/eval_jaxpr/ppermute | solution.py:17
  248.2 7.3 while.78
  256.6 9.0 %collective-permute-done.2 = f32[512]{0:T(512)S(1)} collective-permute-done((f32[512]{0:T(512)S(1)}, f32[512]{0:T(512)S(1)}, u32[]{:S(2)}, u32[]{:S(2)}) %collective-permute-start.2) | collective-permute-done | bytes 2080 | tf_op jit(solution)/shard_map/while/body/eval_jaxpr/ppermute | solution.py:17
  266.8 7.3 while.78
  275.3 9.0 %collective-permute-done.2 = f32[512]{0:T(512)S(1)} collective-permute-done((f32[512]{0:T(512)S(1)}, f32[512]{0:T(512)S(1)}, u32[]{:S(2)}, u32[]{:S(2)}) %collective-permute-start.2) | collective-permute-done | bytes 2080 | tf_op jit(solution)/shard_map/while/body/eval_jaxpr/ppermute | solution.py:17
  285.5 7.3 while.78
  293.9 9.0 %collective-permute-done.2 = f32[512]{0:T(512)S(1)} collective-permute-done((f32[512]{0:T(512)S(1)}, f32[512]{0:T(512)S(1)}, u32[]{:S(2)}, u32[]{:S(2)}) %collective-permute-start.2) | collective-permute-done | bytes 2080 | tf_op jit(solution)/shard_map/while/body/eval_jaxpr/ppermute | solution.py:17
  304.1 7.3 while.78
  312.6 9.0 %collective-permute-done.2 = f32[512]{0:T(512)S(1)} collective-permute-done((f32[512]{0:T(512)S(1)}, f32[512]{0:T(512)S(1)}, u32[]{:S(2)}, u32[]{:S(2)}) %collective-permute-start.2) | collective-permute-done | bytes 2080 | tf_op jit(solution)/shard_map/while/body/eval_jaxpr/ppermute | solution.py:17
  322.7 7.3 while.78
  331.2 9.0 %collective-permute-done.2 = f32[512]{0:T(512)S(1)} collective-permute-done((f32[512]{0:T(512)S(1)}, f32[512]{0:T(512)S(1)}, u32[]{:S(2)}, u32[]{:S(2)}) %collective-permute-start.2) | collective-permute-done | bytes 2080 | tf_op jit(solution)/shard_map/while/body/eval_jaxpr/ppermute | solution.py:17
  341.4 7.3 while.78
  349.8 9.0 %collective-permute-done.2 = f32[512]{0:T(512)S(1)} collective-permute-done((f32[512]{0:T(512)S(1)}, f32[512]{0:T(512)S(1)}, u32[]{:S(2)}, u32[]{:S(2)}) %collective-permute-start.2) | collective-permute-done | bytes 2080 | tf_op jit(solution)/shard_map/while/body/eval_jaxpr/ppermute | solution.py:17
  368.5 9.0 %collective-permute-done.2 = f32[512]{0:T(512)S(1)} collective-permute-done((f32[512]{0:T(512)S(1)}, f32[512]{0:T(512)S(1)}, u32[]{:S(2)}, u32[]{:S(2)}) %collective-permute-start.2) | collective-permute-done | bytes 2080 | tf_op jit(solution)/shard_map/while/body/eval_jaxpr/ppermute | solution.py:17
  387.1 9.0 %collective-permute-done.2 = f32[512]{0:T(512)S(1)} collective-permute-done((f32[512]{0:T(512)S(1)}, f32[512]{0:T(512)S(1)}, u32[]{:S(2)}, u32[]{:S(2)}) %collective-permute-start.2) | collective-permute-done | bytes 2080 | tf_op jit(solution)/shard_map/while/body/eval_jaxpr/ppermute | solution.py:17
  405.7 9.0 %collective-permute-done.2 = f32[512]{0:T(512)S(1)} collective-permute-done((f32[512]{0:T(512)S(1)}, f32[512]{0:T(512)S(1)}, u32[]{:S(2)}, u32[]{:S(2)}) %collective-permute-start.2) | collective-permute-done | bytes 2080 | tf_op jit(solution)/shard_map/while/body/eval_jaxpr/ppermute | solution.py:17
  424.4 9.0 %collective-permute-done.2 = f32[512]{0:T(512)S(1)} collective-permute-done((f32[512]{0:T(512)S(1)}, f32[512]{0:T(512)S(1)}, u32[]{:S(2)}, u32[]{:S(2)}) %collective-permute-start.2) | collective-permute-done | bytes 2080 | tf_op jit(solution)/shard_map/while/body/eval_jaxpr/ppermute | solution.py:17
  443.0 9.0 %collective-permute-done.2 = f32[512]{0:T(512)S(1)} collective-permute-done((f32[512]{0:T(512)S(1)}, f32[512]{0:T(512)S(1)}, u32[]{:S(2)}, u32[]{:S(2)}) %collective-permute-start.2) | collective-permute-done | bytes 2080 | tf_op jit(solution)/shard_map/while/body/eval_jaxpr/ppermute | solution.py:17
  461.6 9.0 %collective-permute-done.2 = f32[512]{0:T(512)S(1)} collective-permute-done((f32[512]{0:T(512)S(1)}, f32[512]{0:T(512)S(1)}, u32[]{:S(2)}, u32[]{:S(2)}) %collective-permute-start.2) | collective-permute-done | bytes 2080 | tf_op jit(solution)/shard_map/while/body/eval_jaxpr/ppermute | solution.py:17
  480.3 9.0 %collective-permute-done.2 = f32[512]{0:T(512)S(1)} collective-permute-done((f32[512]{0:T(512)S(1)}, f32[512]{0:T(512)S(1)}, u32[]{:S(2)}, u32[]{:S(2)}) %collective-permute-start.2) | collective-permute-done | bytes 2080 | tf_op jit(solution)/shard_map/while/body/eval_jaxpr/ppermute | solution.py:17
  498.9 9.0 %collective-permute-done.2 = f32[512]{0:T(512)S(1)} collective-permute-done((f32[512]{0:T(512)S(1)}, f32[512]{0:T(512)S(1)}, u32[]{:S(2)}, u32[]{:S(2)}) %collective-permute-start.2) | collective-permute-done | bytes 2080 | tf_op jit(solution)/shard_map/while/body/eval_jaxpr/ppermute | solution.py:17
  517.5 9.0 %collective-permute-done.2 = f32[512]{0:T(512)S(1)} collective-permute-done((f32[512]{0:T(512)S(1)}, f32[512]{0:T(512)S(1)}, u32[]{:S(2)}, u32[]{:S(2)}) %collective-permute-start.2) | collective-permute-done | bytes 2080 | tf_op jit(solution)/shard_map/while/body/eval_jaxpr/ppermute | solution.py:17
  536.2 9.0 %collective-permute-done.2 = f32[512]{0:T(512)S(1)} collective-permute-done((f32[512]{0:T(512)S(1)}, f32[512]{0:T(512)S(1)}, u32[]{:S(2)}, u32[]{:S(2)}) %collective-permute-start.2) | collective-permute-done | bytes 2080 | tf_op jit(solution)/shard_map/while/body/eval_jaxpr/ppermute | solution.py:17
  554.8 9.0 %collective-permute-done.2 = f32[512]{0:T(512)S(1)} collective-permute-done((f32[512]{0:T(512)S(1)}, f32[512]{0:T(512)S(1)}, u32[]{:S(2)}, u32[]{:S(2)}) %collective-permute-start.2) | collective-permute-done | bytes 2080 | tf_op jit(solution)/shard_map/while/body/eval_jaxpr/ppermute | solution.py:17
  573.5 9.0 %collective-permute-done.2 = f32[512]{0:T(512)S(1)} collective-permute-done((f32[512]{0:T(512)S(1)}, f32[512]{0:T(512)S(1)}, u32[]{:S(2)}, u32[]{:S(2)}) %collective-permute-start.2) | collective-permute-done | bytes 2080 | tf_op jit(solution)/shard_map/while/body/eval_jaxpr/ppermute | solution.py:17
  592.1 9.0 %collective-permute-done.2 = f32[512]{0:T(512)S(1)} collective-permute-done((f32[512]{0:T(512)S(1)}, f32[512]{0:T(512)S(1)}, u32[]{:S(2)}, u32[]{:S(2)}) %collective-permute-start.2) | collective-permute-done | bytes 2080 | tf_op jit(solution)/shard_map/while/body/eval_jaxpr/ppermute | solution.py:17
  602.1 75.3 %all-gather.2.cloned.1.call-done = bf16[2048,1024]{1,0:T(8,128)(2,1)} async-done(((bf16[64,1024]{1,0:T(8,128)(2,1)}), bf16[2048,1024]{1,0:T(8,128)(2,1)}) %all-gather.2.cloned.1.call-update) | async-done | bytes 4194320 | tf_op jit(solution)/shard_map/all_gather | solution.py:123
  682.2 78.3 %reduce-scatter.2.cloned.1.call-done = f32[256,256]{1,0:T(8,128)} async-done(((f32[2048,256]{1,0:T(8,128)}), f32[256,256]{1,0:T(8,128)}) %reduce-scatter.2.cloned.1.call-update) | async-done | bytes 262160 | tf_op jit(solution)/shard_map/reduce_scatter | solution.py:124
  (1090 shorter events, 454.1 us)
Async XLA Ops:
  6.5 670.9 %all-gather.2.cloned.1.call-start = ((), (), s32[]{:S(2)}) async-start(), calls=%async_computation.1 | async-start | bytes 4325376 | tf_op jit(solution)/shard_map/all_gather | solution.py:123
  69.9 9.4 %collective-permute-start.1 = (f32[512,128]{1,0:T(8,128)S(1)}, f32[512,128]{1,0:T(8,128)S(1)}, u32[]{:S(2)}, u32[]{:S(2)}) collective-permute-start(f32[512,128]{1,0:T(8,128)S(1)} %fusion.36), channel_id=1, source_target_pairs={{0,8},{8,16},{16,24},{24,32},{32,40},{40,48},{48,56},{56,64},{64,7... | collective-permute-start | bytes 786440 | tf_op jit(solution)/shard_map/while/body/eval_jaxpr/ppermute | solution.py:17
  88.6 9.4 %collective-permute-start.1 = (f32[512,128]{1,0:T(8,128)S(1)}, f32[512,128]{1,0:T(8,128)S(1)}, u32[]{:S(2)}, u32[]{:S(2)}) collective-permute-start(f32[512,128]{1,0:T(8,128)S(1)} %fusion.36), channel_id=1, source_target_pairs={{0,8},{8,16},{16,24},{24,32},{32,40},{40,48},{48,56},{56,64},{64,7... | collective-permute-start | bytes 786440 | tf_op jit(solution)/shard_map/while/body/eval_jaxpr/ppermute | solution.py:17
  88.6 9.3 %collective-permute-start = (bf16[64,1024]{1,0:T(8,128)(2,1)S(1)}, bf16[64,1024]{1,0:T(8,128)(2,1)S(1)}, u32[]{:S(2)}, u32[]{:S(2)}) collective-permute-start(bf16[64,1024]{1,0:T(8,128)(2,1)S(1)} %copy.27), channel_id=1, source_target_pairs={{0,8},{8,16},{16,24},{24,32},{32,40},{40,48},{48,56},{56,64},{64,7... | collective-permute-start | bytes 393224 | tf_op jit(solution)/shard_map/while/body/eval_jaxpr/ppermute | solution.py:17
  107.2 9.4 %collective-permute-start.1 = (f32[512,128]{1,0:T(8,128)S(1)}, f32[512,128]{1,0:T(8,128)S(1)}, u32[]{:S(2)}, u32[]{:S(2)}) collective-permute-start(f32[512,128]{1,0:T(8,128)S(1)} %fusion.36), channel_id=1, source_target_pairs={{0,8},{8,16},{16,24},{24,32},{32,40},{40,48},{48,56},{56,64},{64,7... | collective-permute-start | bytes 786440 | tf_op jit(solution)/shard_map/while/body/eval_jaxpr/ppermute | solution.py:17
  107.3 9.3 %collective-permute-start = (bf16[64,1024]{1,0:T(8,128)(2,1)S(1)}, bf16[64,1024]{1,0:T(8,128)(2,1)S(1)}, u32[]{:S(2)}, u32[]{:S(2)}) collective-permute-start(bf16[64,1024]{1,0:T(8,128)(2,1)S(1)} %copy.27), channel_id=1, source_target_pairs={{0,8},{8,16},{16,24},{24,32},{32,40},{40,48},{48,56},{56,64},{64,7... | collective-permute-start | bytes 393224 | tf_op jit(solution)/shard_map/while/body/eval_jaxpr/ppermute | solution.py:17
  125.8 9.4 %collective-permute-start.1 = (f32[512,128]{1,0:T(8,128)S(1)}, f32[512,128]{1,0:T(8,128)S(1)}, u32[]{:S(2)}, u32[]{:S(2)}) collective-permute-start(f32[512,128]{1,0:T(8,128)S(1)} %fusion.36), channel_id=1, source_target_pairs={{0,8},{8,16},{16,24},{24,32},{32,40},{40,48},{48,56},{56,64},{64,7... | collective-permute-start | bytes 786440 | tf_op jit(solution)/shard_map/while/body/eval_jaxpr/ppermute | solution.py:17
  125.9 9.3 %collective-permute-start = (bf16[64,1024]{1,0:T(8,128)(2,1)S(1)}, bf16[64,1024]{1,0:T(8,128)(2,1)S(1)}, u32[]{:S(2)}, u32[]{:S(2)}) collective-permute-start(bf16[64,1024]{1,0:T(8,128)(2,1)S(1)} %copy.27), channel_id=1, source_target_pairs={{0,8},{8,16},{16,24},{24,32},{32,40},{40,48},{48,56},{56,64},{64,7... | collective-permute-start | bytes 393224 | tf_op jit(solution)/shard_map/while/body/eval_jaxpr/ppermute | solution.py:17
  144.5 9.4 %collective-permute-start.1 = (f32[512,128]{1,0:T(8,128)S(1)}, f32[512,128]{1,0:T(8,128)S(1)}, u32[]{:S(2)}, u32[]{:S(2)}) collective-permute-start(f32[512,128]{1,0:T(8,128)S(1)} %fusion.36), channel_id=1, source_target_pairs={{0,8},{8,16},{16,24},{24,32},{32,40},{40,48},{48,56},{56,64},{64,7... | collective-permute-start | bytes 786440 | tf_op jit(solution)/shard_map/while/body/eval_jaxpr/ppermute | solution.py:17
  144.6 9.3 %collective-permute-start = (bf16[64,1024]{1,0:T(8,128)(2,1)S(1)}, bf16[64,1024]{1,0:T(8,128)(2,1)S(1)}, u32[]{:S(2)}, u32[]{:S(2)}) collective-permute-start(bf16[64,1024]{1,0:T(8,128)(2,1)S(1)} %copy.27), channel_id=1, source_target_pairs={{0,8},{8,16},{16,24},{24,32},{32,40},{40,48},{48,56},{56,64},{64,7... | collective-permute-start | bytes 393224 | tf_op jit(solution)/shard_map/while/body/eval_jaxpr/ppermute | solution.py:17
  163.1 9.4 %collective-permute-start.1 = (f32[512,128]{1,0:T(8,128)S(1)}, f32[512,128]{1,0:T(8,128)S(1)}, u32[]{:S(2)}, u32[]{:S(2)}) collective-permute-start(f32[512,128]{1,0:T(8,128)S(1)} %fusion.36), channel_id=1, source_target_pairs={{0,8},{8,16},{16,24},{24,32},{32,40},{40,48},{48,56},{56,64},{64,7... | collective-permute-start | bytes 786440 | tf_op jit(solution)/shard_map/while/body/eval_jaxpr/ppermute | solution.py:17
  163.2 9.3 %collective-permute-start = (bf16[64,1024]{1,0:T(8,128)(2,1)S(1)}, bf16[64,1024]{1,0:T(8,128)(2,1)S(1)}, u32[]{:S(2)}, u32[]{:S(2)}) collective-permute-start(bf16[64,1024]{1,0:T(8,128)(2,1)S(1)} %copy.27), channel_id=1, source_target_pairs={{0,8},{8,16},{16,24},{24,32},{32,40},{40,48},{48,56},{56,64},{64,7... | collective-permute-start | bytes 393224 | tf_op jit(solution)/shard_map/while/body/eval_jaxpr/ppermute | solution.py:17
  181.7 9.4 %collective-permute-start.1 = (f32[512,128]{1,0:T(8,128)S(1)}, f32[512,128]{1,0:T(8,128)S(1)}, u32[]{:S(2)}, u32[]{:S(2)}) collective-permute-start(f32[512,128]{1,0:T(8,128)S(1)} %fusion.36), channel_id=1, source_target_pairs={{0,8},{8,16},{16,24},{24,32},{32,40},{40,48},{48,56},{56,64},{64,7... | collective-permute-start | bytes 786440 | tf_op jit(solution)/shard_map/while/body/eval_jaxpr/ppermute | solution.py:17
  181.8 9.3 %collective-permute-start = (bf16[64,1024]{1,0:T(8,128)(2,1)S(1)}, bf16[64,1024]{1,0:T(8,128)(2,1)S(1)}, u32[]{:S(2)}, u32[]{:S(2)}) collective-permute-start(bf16[64,1024]{1,0:T(8,128)(2,1)S(1)} %copy.27), channel_id=1, source_target_pairs={{0,8},{8,16},{16,24},{24,32},{32,40},{40,48},{48,56},{56,64},{64,7... | collective-permute-start | bytes 393224 | tf_op jit(solution)/shard_map/while/body/eval_jaxpr/ppermute | solution.py:17
  200.4 9.4 %collective-permute-start.1 = (f32[512,128]{1,0:T(8,128)S(1)}, f32[512,128]{1,0:T(8,128)S(1)}, u32[]{:S(2)}, u32[]{:S(2)}) collective-permute-start(f32[512,128]{1,0:T(8,128)S(1)} %fusion.36), channel_id=1, source_target_pairs={{0,8},{8,16},{16,24},{24,32},{32,40},{40,48},{48,56},{56,64},{64,7... | collective-permute-start | bytes 786440 | tf_op jit(solution)/shard_map/while/body/eval_jaxpr/ppermute | solution.py:17
  200.5 9.3 %collective-permute-start = (bf16[64,1024]{1,0:T(8,128)(2,1)S(1)}, bf16[64,1024]{1,0:T(8,128)(2,1)S(1)}, u32[]{:S(2)}, u32[]{:S(2)}) collective-permute-start(bf16[64,1024]{1,0:T(8,128)(2,1)S(1)} %copy.27), channel_id=1, source_target_pairs={{0,8},{8,16},{16,24},{24,32},{32,40},{40,48},{48,56},{56,64},{64,7... | collective-permute-start | bytes 393224 | tf_op jit(solution)/shard_map/while/body/eval_jaxpr/ppermute | solution.py:17
  219.0 9.4 %collective-permute-start.1 = (f32[512,128]{1,0:T(8,128)S(1)}, f32[512,128]{1,0:T(8,128)S(1)}, u32[]{:S(2)}, u32[]{:S(2)}) collective-permute-start(f32[512,128]{1,0:T(8,128)S(1)} %fusion.36), channel_id=1, source_target_pairs={{0,8},{8,16},{16,24},{24,32},{32,40},{40,48},{48,56},{56,64},{64,7... | collective-permute-start | bytes 786440 | tf_op jit(solution)/shard_map/while/body/eval_jaxpr/ppermute | solution.py:17
  219.1 9.3 %collective-permute-start = (bf16[64,1024]{1,0:T(8,128)(2,1)S(1)}, bf16[64,1024]{1,0:T(8,128)(2,1)S(1)}, u32[]{:S(2)}, u32[]{:S(2)}) collective-permute-start(bf16[64,1024]{1,0:T(8,128)(2,1)S(1)} %copy.27), channel_id=1, source_target_pairs={{0,8},{8,16},{16,24},{24,32},{32,40},{40,48},{48,56},{56,64},{64,7... | collective-permute-start | bytes 393224 | tf_op jit(solution)/shard_map/while/body/eval_jaxpr/ppermute | solution.py:17
  237.6 9.4 %collective-permute-start.1 = (f32[512,128]{1,0:T(8,128)S(1)}, f32[512,128]{1,0:T(8,128)S(1)}, u32[]{:S(2)}, u32[]{:S(2)}) collective-permute-start(f32[512,128]{1,0:T(8,128)S(1)} %fusion.36), channel_id=1, source_target_pairs={{0,8},{8,16},{16,24},{24,32},{32,40},{40,48},{48,56},{56,64},{64,7... | collective-permute-start | bytes 786440 | tf_op jit(solution)/shard_map/while/body/eval_jaxpr/ppermute | solution.py:17
  237.7 9.3 %collective-permute-start = (bf16[64,1024]{1,0:T(8,128)(2,1)S(1)}, bf16[64,1024]{1,0:T(8,128)(2,1)S(1)}, u32[]{:S(2)}, u32[]{:S(2)}) collective-permute-start(bf16[64,1024]{1,0:T(8,128)(2,1)S(1)} %copy.27), channel_id=1, source_target_pairs={{0,8},{8,16},{16,24},{24,32},{32,40},{40,48},{48,56},{56,64},{64,7... | collective-permute-start | bytes 393224 | tf_op jit(solution)/shard_map/while/body/eval_jaxpr/ppermute | solution.py:17
  256.3 9.4 %collective-permute-start.1 = (f32[512,128]{1,0:T(8,128)S(1)}, f32[512,128]{1,0:T(8,128)S(1)}, u32[]{:S(2)}, u32[]{:S(2)}) collective-permute-start(f32[512,128]{1,0:T(8,128)S(1)} %fusion.36), channel_id=1, source_target_pairs={{0,8},{8,16},{16,24},{24,32},{32,40},{40,48},{48,56},{56,64},{64,7... | collective-permute-start | bytes 786440 | tf_op jit(solution)/shard_map/while/body/eval_jaxpr/ppermute | solution.py:17
  256.4 9.3 %collective-permute-start = (bf16[64,1024]{1,0:T(8,128)(2,1)S(1)}, bf16[64,1024]{1,0:T(8,128)(2,1)S(1)}, u32[]{:S(2)}, u32[]{:S(2)}) collective-permute-start(bf16[64,1024]{1,0:T(8,128)(2,1)S(1)} %copy.27), channel_id=1, source_target_pairs={{0,8},{8,16},{16,24},{24,32},{32,40},{40,48},{48,56},{56,64},{64,7... | collective-permute-start | bytes 393224 | tf_op jit(solution)/shard_map/while/body/eval_jaxpr/ppermute | solution.py:17
  274.9 9.4 %collective-permute-start.1 = (f32[512,128]{1,0:T(8,128)S(1)}, f32[512,128]{1,0:T(8,128)S(1)}, u32[]{:S(2)}, u32[]{:S(2)}) collective-permute-start(f32[512,128]{1,0:T(8,128)S(1)} %fusion.36), channel_id=1, source_target_pairs={{0,8},{8,16},{16,24},{24,32},{32,40},{40,48},{48,56},{56,64},{64,7... | collective-permute-start | bytes 786440 | tf_op jit(solution)/shard_map/while/body/eval_jaxpr/ppermute | solution.py:17
  275.0 9.3 %collective-permute-start = (bf16[64,1024]{1,0:T(8,128)(2,1)S(1)}, bf16[64,1024]{1,0:T(8,128)(2,1)S(1)}, u32[]{:S(2)}, u32[]{:S(2)}) collective-permute-start(bf16[64,1024]{1,0:T(8,128)(2,1)S(1)} %copy.27), channel_id=1, source_target_pairs={{0,8},{8,16},{16,24},{24,32},{32,40},{40,48},{48,56},{56,64},{64,7... | collective-permute-start | bytes 393224 | tf_op jit(solution)/shard_map/while/body/eval_jaxpr/ppermute | solution.py:17
  293.6 9.4 %collective-permute-start.1 = (f32[512,128]{1,0:T(8,128)S(1)}, f32[512,128]{1,0:T(8,128)S(1)}, u32[]{:S(2)}, u32[]{:S(2)}) collective-permute-start(f32[512,128]{1,0:T(8,128)S(1)} %fusion.36), channel_id=1, source_target_pairs={{0,8},{8,16},{16,24},{24,32},{32,40},{40,48},{48,56},{56,64},{64,7... | collective-permute-start | bytes 786440 | tf_op jit(solution)/shard_map/while/body/eval_jaxpr/ppermute | solution.py:17
  312.2 9.4 %collective-permute-start.1 = (f32[512,128]{1,0:T(8,128)S(1)}, f32[512,128]{1,0:T(8,128)S(1)}, u32[]{:S(2)}, u32[]{:S(2)}) collective-permute-start(f32[512,128]{1,0:T(8,128)S(1)} %fusion.36), channel_id=1, source_target_pairs={{0,8},{8,16},{16,24},{24,32},{32,40},{40,48},{48,56},{56,64},{64,7... | collective-permute-start | bytes 786440 | tf_op jit(solution)/shard_map/while/body/eval_jaxpr/ppermute | solution.py:17
  312.3 9.3 %collective-permute-start = (bf16[64,1024]{1,0:T(8,128)(2,1)S(1)}, bf16[64,1024]{1,0:T(8,128)(2,1)S(1)}, u32[]{:S(2)}, u32[]{:S(2)}) collective-permute-start(bf16[64,1024]{1,0:T(8,128)(2,1)S(1)} %copy.27), channel_id=1, source_target_pairs={{0,8},{8,16},{16,24},{24,32},{32,40},{40,48},{48,56},{56,64},{64,7... | collective-permute-start | bytes 393224 | tf_op jit(solution)/shard_map/while/body/eval_jaxpr/ppermute | solution.py:17
  330.8 9.4 %collective-permute-start.1 = (f32[512,128]{1,0:T(8,128)S(1)}, f32[512,128]{1,0:T(8,128)S(1)}, u32[]{:S(2)}, u32[]{:S(2)}) collective-permute-start(f32[512,128]{1,0:T(8,128)S(1)} %fusion.36), channel_id=1, source_target_pairs={{0,8},{8,16},{16,24},{24,32},{32,40},{40,48},{48,56},{56,64},{64,7... | collective-permute-start | bytes 786440 | tf_op jit(solution)/shard_map/while/body/eval_jaxpr/ppermute | solution.py:17
  349.5 9.4 %collective-permute-start.1 = (f32[512,128]{1,0:T(8,128)S(1)}, f32[512,128]{1,0:T(8,128)S(1)}, u32[]{:S(2)}, u32[]{:S(2)}) collective-permute-start(f32[512,128]{1,0:T(8,128)S(1)} %fusion.36), channel_id=1, source_target_pairs={{0,8},{8,16},{16,24},{24,32},{32,40},{40,48},{48,56},{56,64},{64,7... | collective-permute-start | bytes 786440 | tf_op jit(solution)/shard_map/while/body/eval_jaxpr/ppermute | solution.py:17
  349.5 9.3 %collective-permute-start = (bf16[64,1024]{1,0:T(8,128)(2,1)S(1)}, bf16[64,1024]{1,0:T(8,128)(2,1)S(1)}, u32[]{:S(2)}, u32[]{:S(2)}) collective-permute-start(bf16[64,1024]{1,0:T(8,128)(2,1)S(1)} %copy.27), channel_id=1, source_target_pairs={{0,8},{8,16},{16,24},{24,32},{32,40},{40,48},{48,56},{56,64},{64,7... | collective-permute-start | bytes 393224 | tf_op jit(solution)/shard_map/while/body/eval_jaxpr/ppermute | solution.py:17
  368.1 9.4 %collective-permute-start.1 = (f32[512,128]{1,0:T(8,128)S(1)}, f32[512,128]{1,0:T(8,128)S(1)}, u32[]{:S(2)}, u32[]{:S(2)}) collective-permute-start(f32[512,128]{1,0:T(8,128)S(1)} %fusion.36), channel_id=1, source_target_pairs={{0,8},{8,16},{16,24},{24,32},{32,40},{40,48},{48,56},{56,64},{64,7... | collective-permute-start | bytes 786440 | tf_op jit(solution)/shard_map/while/body/eval_jaxpr/ppermute | solution.py:17
  386.7 9.4 %collective-permute-start.1 = (f32[512,128]{1,0:T(8,128)S(1)}, f32[512,128]{1,0:T(8,128)S(1)}, u32[]{:S(2)}, u32[]{:S(2)}) collective-permute-start(f32[512,128]{1,0:T(8,128)S(1)} %fusion.36), channel_id=1, source_target_pairs={{0,8},{8,16},{16,24},{24,32},{32,40},{40,48},{48,56},{56,64},{64,7... | collective-permute-start | bytes 786440 | tf_op jit(solution)/shard_map/while/body/eval_jaxpr/ppermute | solution.py:17
  386.8 9.3 %collective-permute-start = (bf16[64,1024]{1,0:T(8,128)(2,1)S(1)}, bf16[64,1024]{1,0:T(8,128)(2,1)S(1)}, u32[]{:S(2)}, u32[]{:S(2)}) collective-permute-start(bf16[64,1024]{1,0:T(8,128)(2,1)S(1)} %copy.27), channel_id=1, source_target_pairs={{0,8},{8,16},{16,24},{24,32},{32,40},{40,48},{48,56},{56,64},{64,7... | collective-permute-start | bytes 393224 | tf_op jit(solution)/shard_map/while/body/eval_jaxpr/ppermute | solution.py:17
  405.4 9.4 %collective-permute-start.1 = (f32[512,128]{1,0:T(8,128)S(1)}, f32[512,128]{1,0:T(8,128)S(1)}, u32[]{:S(2)}, u32[]{:S(2)}) collective-permute-start(f32[512,128]{1,0:T(8,128)S(1)} %fusion.36), channel_id=1, source_target_pairs={{0,8},{8,16},{16,24},{24,32},{32,40},{40,48},{48,56},{56,64},{64,7... | collective-permute-start | bytes 786440 | tf_op jit(solution)/shard_map/while/body/eval_jaxpr/ppermute | solution.py:17
  424.0 9.4 %collective-permute-start.1 = (f32[512,128]{1,0:T(8,128)S(1)}, f32[512,128]{1,0:T(8,128)S(1)}, u32[]{:S(2)}, u32[]{:S(2)}) collective-permute-start(f32[512,128]{1,0:T(8,128)S(1)} %fusion.36), channel_id=1, source_target_pairs={{0,8},{8,16},{16,24},{24,32},{32,40},{40,48},{48,56},{56,64},{64,7... | collective-permute-start | bytes 786440 | tf_op jit(solution)/shard_map/while/body/eval_jaxpr/ppermute | solution.py:17
  424.1 9.3 %collective-permute-start = (bf16[64,1024]{1,0:T(8,128)(2,1)S(1)}, bf16[64,1024]{1,0:T(8,128)(2,1)S(1)}, u32[]{:S(2)}, u32[]{:S(2)}) collective-permute-start(bf16[64,1024]{1,0:T(8,128)(2,1)S(1)} %copy.27), channel_id=1, source_target_pairs={{0,8},{8,16},{16,24},{24,32},{32,40},{40,48},{48,56},{56,64},{64,7... | collective-permute-start | bytes 393224 | tf_op jit(solution)/shard_map/while/body/eval_jaxpr/ppermute | solution.py:17
  442.6 9.4 %collective-permute-start.1 = (f32[512,128]{1,0:T(8,128)S(1)}, f32[512,128]{1,0:T(8,128)S(1)}, u32[]{:S(2)}, u32[]{:S(2)}) collective-permute-start(f32[512,128]{1,0:T(8,128)S(1)} %fusion.36), channel_id=1, source_target_pairs={{0,8},{8,16},{16,24},{24,32},{32,40},{40,48},{48,56},{56,64},{64,7... | collective-permute-start | bytes 786440 | tf_op jit(solution)/shard_map/while/body/eval_jaxpr/ppermute | solution.py:17
  461.3 9.4 %collective-permute-start.1 = (f32[512,128]{1,0:T(8,128)S(1)}, f32[512,128]{1,0:T(8,128)S(1)}, u32[]{:S(2)}, u32[]{:S(2)}) collective-permute-start(f32[512,128]{1,0:T(8,128)S(1)} %fusion.36), channel_id=1, source_target_pairs={{0,8},{8,16},{16,24},{24,32},{32,40},{40,48},{48,56},{56,64},{64,7... | collective-permute-start | bytes 786440 | tf_op jit(solution)/shard_map/while/body/eval_jaxpr/ppermute | solution.py:17
  461.4 9.3 %collective-permute-start = (bf16[64,1024]{1,0:T(8,128)(2,1)S(1)}, bf16[64,1024]{1,0:T(8,128)(2,1)S(1)}, u32[]{:S(2)}, u32[]{:S(2)}) collective-permute-start(bf16[64,1024]{1,0:T(8,128)(2,1)S(1)} %copy.27), channel_id=1, source_target_pairs={{0,8},{8,16},{16,24},{24,32},{32,40},{40,48},{48,56},{56,64},{64,7... | collective-permute-start | bytes 393224 | tf_op jit(solution)/shard_map/while/body/eval_jaxpr/ppermute | solution.py:17
  479.9 9.4 %collective-permute-start.1 = (f32[512,128]{1,0:T(8,128)S(1)}, f32[512,128]{1,0:T(8,128)S(1)}, u32[]{:S(2)}, u32[]{:S(2)}) collective-permute-start(f32[512,128]{1,0:T(8,128)S(1)} %fusion.36), channel_id=1, source_target_pairs={{0,8},{8,16},{16,24},{24,32},{32,40},{40,48},{48,56},{56,64},{64,7... | collective-permute-start | bytes 786440 | tf_op jit(solution)/shard_map/while/body/eval_jaxpr/ppermute | solution.py:17
  498.5 9.4 %collective-permute-start.1 = (f32[512,128]{1,0:T(8,128)S(1)}, f32[512,128]{1,0:T(8,128)S(1)}, u32[]{:S(2)}, u32[]{:S(2)}) collective-permute-start(f32[512,128]{1,0:T(8,128)S(1)} %fusion.36), channel_id=1, source_target_pairs={{0,8},{8,16},{16,24},{24,32},{32,40},{40,48},{48,56},{56,64},{64,7... | collective-permute-start | bytes 786440 | tf_op jit(solution)/shard_map/while/body/eval_jaxpr/ppermute | solution.py:17
  498.6 9.3 %collective-permute-start = (bf16[64,1024]{1,0:T(8,128)(2,1)S(1)}, bf16[64,1024]{1,0:T(8,128)(2,1)S(1)}, u32[]{:S(2)}, u32[]{:S(2)}) collective-permute-start(bf16[64,1024]{1,0:T(8,128)(2,1)S(1)} %copy.27), channel_id=1, source_target_pairs={{0,8},{8,16},{16,24},{24,32},{32,40},{40,48},{48,56},{56,64},{64,7... | collective-permute-start | bytes 393224 | tf_op jit(solution)/shard_map/while/body/eval_jaxpr/ppermute | solution.py:17
  517.2 9.4 %collective-permute-start.1 = (f32[512,128]{1,0:T(8,128)S(1)}, f32[512,128]{1,0:T(8,128)S(1)}, u32[]{:S(2)}, u32[]{:S(2)}) collective-permute-start(f32[512,128]{1,0:T(8,128)S(1)} %fusion.36), channel_id=1, source_target_pairs={{0,8},{8,16},{16,24},{24,32},{32,40},{40,48},{48,56},{56,64},{64,7... | collective-permute-start | bytes 786440 | tf_op jit(solution)/shard_map/while/body/eval_jaxpr/ppermute | solution.py:17
  535.8 9.4 %collective-permute-start.1 = (f32[512,128]{1,0:T(8,128)S(1)}, f32[512,128]{1,0:T(8,128)S(1)}, u32[]{:S(2)}, u32[]{:S(2)}) collective-permute-start(f32[512,128]{1,0:T(8,128)S(1)} %fusion.36), channel_id=1, source_target_pairs={{0,8},{8,16},{16,24},{24,32},{32,40},{40,48},{48,56},{56,64},{64,7... | collective-permute-start | bytes 786440 | tf_op jit(solution)/shard_map/while/body/eval_jaxpr/ppermute | solution.py:17
  554.5 9.4 %collective-permute-start.1 = (f32[512,128]{1,0:T(8,128)S(1)}, f32[512,128]{1,0:T(8,128)S(1)}, u32[]{:S(2)}, u32[]{:S(2)}) collective-permute-start(f32[512,128]{1,0:T(8,128)S(1)} %fusion.36), channel_id=1, source_target_pairs={{0,8},{8,16},{16,24},{24,32},{32,40},{40,48},{48,56},{56,64},{64,7... | collective-permute-start | bytes 786440 | tf_op jit(solution)/shard_map/while/body/eval_jaxpr/ppermute | solution.py:17
  573.1 9.4 %collective-permute-start.1 = (f32[512,128]{1,0:T(8,128)S(1)}, f32[512,128]{1,0:T(8,128)S(1)}, u32[]{:S(2)}, u32[]{:S(2)}) collective-permute-start(f32[512,128]{1,0:T(8,128)S(1)} %fusion.36), channel_id=1, source_target_pairs={{0,8},{8,16},{16,24},{24,32},{32,40},{40,48},{48,56},{56,64},{64,7... | collective-permute-start | bytes 786440 | tf_op jit(solution)/shard_map/while/body/eval_jaxpr/ppermute | solution.py:17
  591.7 9.4 %collective-permute-start.1 = (f32[512,128]{1,0:T(8,128)S(1)}, f32[512,128]{1,0:T(8,128)S(1)}, u32[]{:S(2)}, u32[]{:S(2)}) collective-permute-start(f32[512,128]{1,0:T(8,128)S(1)} %fusion.36), channel_id=1, source_target_pairs={{0,8},{8,16},{16,24},{24,32},{32,40},{40,48},{48,56},{56,64},{64,7... | collective-permute-start | bytes 786440 | tf_op jit(solution)/shard_map/while/body/eval_jaxpr/ppermute | solution.py:17
  602.0 158.5 %reduce-scatter.2.cloned.1.call-start = ((), (), s32[]{:S(2)}) async-start(), calls=%async_computation.2 | async-start | bytes 2359296 | tf_op jit(solution)/shard_map/reduce_scatter | solution.py:124
  (147 other events, 1843.4 us)
Sparse Core Ops, SparseCore 0:
  602.2 75.1 all-gather.1
  682.3 78.1 reduce-scatter.1
where the time goes:
time: 775 us; the launch traced here: 769 us
  waiting for transfers between devices  411 us (53%)
  matrix products  199 us (26%)
  other arithmetic  62.1 us (8%)
  starting transfers between devices  38.9 us (5%)
  local copies, waits for them, and re-layouts  35.7 us (5%)
  between operations  14.1 us (2%)
  loops' own time  8.03 us (1%)
    ppermute x128, waiting for transfers between devices, shifted(): return lax.ppermute(value, axis, pairs)  258 us
    dot_general x96, matrix products, block_terms(): summed = jnp.dot(weights, value_rows, preferred_element_type=jnp.float32)  110 us
    dot_general x96, matrix products, block_terms(): jnp.dot(query_rows, key_rows.T, preferred_element_type=jnp.float32)  84.6 us
    reduce_scatter x1, waiting for transfers between devices, body(): lax.psum_scatter(jnp.dot(attended_every, out_weight, preferred_element_ty...  78.3 us
    all_gather x1, waiting for transfers between devices, body(): attended_every = lax.all_gather(attended, 'seq', axis=0, tiled=True)  75.3 us
    lt x64, other arithmetic, visit(): usable = offset + jnp.arange(BLOCK, dtype=jnp.int32) < length  41.8 us
    ppermute x128, starting transfers between devices, shifted(): return lax.ppermute(value, axis, pairs)  38.9 us
    dynamic_slice x32, local copies, waits for them, and re-layouts, anchor_rank(): lax.dynamic_slice_in_dim(span_rank, anchor * tokens, tokens)  24.5 us
  transfers between devices with their start and end apart: 130, of which 34 were waited for; matrix products, arithmetic and copies ran while one was open for 0% of the time, Pallas kernels for 0%

commit v1 on v0

v1 whole, which is shorter than its diff:
```python
import functools
import math

import jax
import jax.numpy as jnp
from jax import lax
from jax.experimental import pallas as pl
from jax.experimental.pallas import tpu as pltpu
from jax.sharding import PartitionSpec as P

NEG_FILL = -1e30
BF16 = jnp.bfloat16
F32 = jnp.float32
Z, YC, HEADS = 8, 4, 8
QPH, HD = 8, 128
TOK = 64
CACHE = 1024
GRAN = 128
CHUNK = 1024
SHARDS = 8
ROWS = TOK * QPH
VROWS = 144
WIDE = QPH * HD + 128
META = 2 * CACHE + 2 * TOK
BLOCK_ROWS = META + 16
KEYS = SHARDS * CACHE + CHUNK


def seq_permute(value, move):
    pairs = []
    for z in range(Z):
        for y in range(2):
            for c in range(2):
                to_z, to_y, to_c = move(z, y, c)
                pairs.append((z * 4 + y * 2 + c, (to_z % Z) * 4 + to_y * 2 + to_c))
    return lax.ppermute(value, "seq", pairs)


def attention_kernel(*refs):
    q_refs, kv_refs = refs[:4], refs[4:12]
    q_rank, k_rank = refs[12:14]
    outs = refs[14:18]
    q_all, k_all, v_all, new_k, new_v, m_all, acc = refs[18:]
    factor = F32(math.log2(math.e) / math.sqrt(HD))
    for b in range(4):
        for h in range(QPH):
            scaled = q_refs[b][:, h * HD : (h + 1) * HD].astype(F32) * factor
            high = scaled.astype(BF16)
            rows = pl.ds(b * ROWS + h * TOK, TOK)
            q_all[rows, 0:HD] = high
            q_all[rows, HD : 2 * HD] = (scaled - high.astype(F32)).astype(BF16)
    m_all[...] = jnp.full(m_all.shape, NEG_FILL, F32)
    acc[...] = jnp.zeros(acc.shape, F32)

    ones16 = (lax.broadcasted_iota(jnp.int32, (16, CACHE), 0) == 0).astype(F32)
    position = lax.broadcasted_iota(jnp.int32, (CACHE, HD), 0)
    lane_position = lax.broadcasted_iota(jnp.int32, (16, CACHE), 1)
    total = jnp.int32(0)
    for s in range(SHARDS):
        ref = kv_refs[s]
        meta = ref[META : META + 16, :].astype(F32).astype(jnp.int32)
        length = jnp.max(meta[0:8, :]) * 32 + jnp.max(meta[8:16, :])
        start = pl.multiple_of(total, GRAN)
        counted = position < length
        keys = ref[0:CACHE, :]
        keys = jnp.where(counted, keys, jnp.broadcast_to(keys[0:1, :], keys.shape))
        k_all[pl.ds(start, CACHE), 0:HD] = keys
        k_all[pl.ds(start, CACHE), HD : 2 * HD] = keys
        values = ref[CACHE : 2 * CACHE, :]
        values = jnp.where(counted, values, jnp.zeros_like(values))
        v_all[0:HD, pl.ds(start, CACHE)] = values.T
        flags = jnp.where(lane_position < length, ones16, 0.0).astype(BF16)
        v_all[HD:VROWS, pl.ds(start, CACHE)] = flags
        total = total + ((length + GRAN - 1) // GRAN) * GRAN
        rows = pl.ds(s * TOK, TOK)
        fresh = ref[2 * CACHE : 2 * CACHE + TOK, :]
        new_k[rows, 0:HD] = fresh
        new_k[rows, HD : 2 * HD] = fresh
        new_v[rows, :] = ref[2 * CACHE + TOK : META, :]
    filler = pl.ds(pl.multiple_of(total, GRAN), CHUNK)
    k_all[filler, :] = jnp.broadcast_to(k_all[0:1, :], (CHUNK, 2 * HD))
    v_all[:, filler] = jnp.zeros((VROWS, CHUNK), BF16)

    def scores(k, b):
        return lax.dot_general(
            k, q_all[b * ROWS : (b + 1) * ROWS, :], (((1,), (1,)), ((), ())),
            preferred_element_type=F32,
        )

    def weigh(s, b):
        cols = slice(b * ROWS, (b + 1) * ROWS)
        before = m_all[:, cols]
        top = jnp.maximum(before, jnp.max(s, axis=0, keepdims=True))
        m_all[:, cols] = top
        return jnp.exp2(s - top).astype(BF16), jnp.exp2(before - top)

    def add(p, scale, v, b):
        cols = slice(b * ROWS, (b + 1) * ROWS)
        acc[:, cols] = acc[:, cols] * scale + jnp.dot(v, p, preferred_element_type=F32)

    def step(k, v, mask=None):
        s = scores(k, 0)
        held = None
        for b in range(4):
            following = scores(k, b + 1) if b < 3 else None
            if mask is not None:
                s = jnp.where(mask(b), s, NEG_FILL)
            p, scale = weigh(s, b)
            if held is not None:
                add(*held)
            held = (p, scale, v, b)
            s = following
        add(*held)

    def cached(start, size):
        start = pl.multiple_of(start, GRAN)
        step(k_all[pl.ds(start, size), :], v_all[:, pl.ds(start, size)])

    whole = total // CHUNK
    rest = total - whole * CHUNK

    @pl.loop(0, whole)
    def _(i):
        cached(i * CHUNK, CHUNK)

    @pl.when(jnp.logical_and(rest > 0, rest <= CHUNK // 2))
    def _():
        cached(whole * CHUNK, CHUNK // 2)

    @pl.when(rest > CHUNK // 2)
    def _():
        cached(whole * CHUNK, CHUNK)

    new_vt = jnp.concatenate(
        [new_v[...].T, ones16[:, 0 : SHARDS * TOK].astype(BF16)], axis=0
    )
    step(
        new_k[...],
        new_vt,
        lambda b: k_rank[:, 0:1] <= q_rank[b : b + 1, :],
    )

    for b in range(4):
        stats = []
        for h in range(QPH):
            cols = slice(b * ROWS + h * TOK, b * ROWS + (h + 1) * TOK)
            held = acc[:, cols]
            weight = held[HD : HD + 1, :]
            outs[b][:, h * HD : (h + 1) * HD] = (held[0:HD, :] / weight).T.astype(BF16)
            stats.append(m_all[:, cols] + jnp.log2(weight))
        stats = jnp.concatenate(stats, axis=0)
        high = stats.astype(BF16).astype(F32)
        middle = (stats - high).astype(BF16).astype(F32)
        low = stats - high - middle
        stats = jnp.concatenate([high, middle, low, jnp.zeros((104, TOK), F32)], axis=0)
        outs[b][:, QPH * HD : WIDE] = stats.T.astype(BF16)


def attention(q_blocks, kv_blocks, q_rank, k_rank):
    return pl.pallas_call(
        attention_kernel,
        out_shape=[jax.ShapeDtypeStruct((TOK, WIDE), BF16)] * 4,
        scratch_shapes=[
            pltpu.VMEM((4 * ROWS, 2 * HD), BF16),
            pltpu.VMEM((KEYS, 2 * HD), BF16),
            pltpu.VMEM((VROWS, KEYS), BF16),
            pltpu.VMEM((SHARDS * TOK, 2 * HD), BF16),
            pltpu.VMEM((SHARDS * TOK, HD), BF16),
            pltpu.VMEM((1, 4 * ROWS), F32),
            pltpu.VMEM((VROWS, 4 * ROWS), F32),
        ],
        compiler_params=pltpu.CompilerParams(vmem_limit_bytes=56 * 2**20),
        name="attention",
    )(*q_blocks, *kv_blocks, q_rank, k_rank)


def merge_kernel(a_ref, b_ref, c_ref, d_ref, out_ref):
    parts = (a_ref, b_ref, c_ref, d_ref)
    stats = []
    for part in parts:
        lanes = part[:, QPH * HD : WIDE].astype(F32)
        stats.append(lanes[:, 0:8] + lanes[:, 8:16] + lanes[:, 16:24])
    top = functools.reduce(jnp.maximum, stats)
    shares = [jnp.exp2(s - top) for s in stats]
    whole = functools.reduce(jnp.add, shares)
    shares = [s / whole for s in shares]
    for h in range(QPH):
        cols = slice(h * HD, (h + 1) * HD)
        out_ref[:, cols] = functools.reduce(
            jnp.add,
            [p[:, cols].astype(F32) * s[:, h : h + 1] for p, s in zip(parts, shares)],
        ).astype(BF16)


def merge(parts):
    return pl.pallas_call(
        merge_kernel,
        out_shape=jax.ShapeDtypeStruct((TOK, QPH * HD), BF16),
        name="merge",
    )(*parts)


def body(queries, cache_keys, cache_values, new_keys, new_values, cache_len, span_rank, out_weight):
    seq = lax.axis_index("seq")
    z, yc = seq // 4, seq % 4
    y, c = yc // 2, yc % 2

    length = cache_len[0]
    meta = jnp.where(jnp.arange(16)[:, None] < 8, length // 32, length % 32)
    meta = jnp.broadcast_to(meta, (16, HD)).astype(BF16)
    own = jnp.concatenate([cache_keys[0], cache_values[0], new_keys, new_values, meta], axis=0)

    over_c = lambda v: seq_permute(v, lambda z, y, c: (z, y, 1 - c))
    kv_y = seq_permute(own, lambda z, y, c: (z, 1 - y, c))
    kv_z = seq_permute(own, lambda z, y, c: (z ^ 1, y, c))
    q_up = seq_permute(queries, lambda z, y, c: (z - 2, y, c))
    q_down = seq_permute(queries, lambda z, y, c: (z + 2, y, c))
    q_far = seq_permute(queries, lambda z, y, c: (z + 4, y, c))
    kv_yz = seq_permute(own, lambda z, y, c: (z ^ 1, 1 - y, c))
    kv = []
    for block in (own, kv_y, kv_z, kv_yz):
        kv += [block, over_c(block)]

    ranks = span_rank.reshape(Z, 2, 2, TOK)
    flip = lambda a, on, dim: jnp.where(on == 1, jnp.flip(a, dim), a)
    near = lax.dynamic_slice_in_dim(ranks, (z // 2) * 2, 2, 0)
    near = flip(flip(flip(near, z % 2, 0), y, 1), c, 2)
    k_rank = jnp.stack([near[0, 0], near[0, 1], near[1, 0], near[1, 1]]).reshape(SHARDS * TOK, 1)
    k_rank = jnp.broadcast_to(k_rank, (SHARDS * TOK, HD))
    by_z = lax.dynamic_index_in_dim(span_rank.reshape(Z, YC, TOK), yc, 1, False)
    steps = (z + jnp.array([4, 2, 6, 0])) % Z
    q_rank = jnp.tile(by_z[steps], (1, QPH))

    far, up, down, mine = attention((q_far, q_up, q_down, queries), kv, q_rank, k_rank)
    from_far = seq_permute(far, lambda z, y, c: (z + 4, y, c))
    from_down = seq_permute(up, lambda z, y, c: (z + 2, y, c))
    from_up = seq_permute(down, lambda z, y, c: (z - 2, y, c))
    attended = merge((from_far, from_down, from_up, mine))

    planes = [[z * 4 + i for i in range(YC)] for z in range(Z)]
    columns = [[z * 4 + i for z in range(Z)] for i in range(YC)]
    weights = lax.all_gather(out_weight, "seq", axis=0, axis_index_groups=columns)
    plane = lax.all_gather(attended, "seq", axis=0, tiled=True, axis_index_groups=planes)
    shares = jnp.einsum("tf,zfc->ztc", plane, weights, preferred_element_type=F32).astype(BF16)
    shares = lax.all_to_all(shares, "head", 0, 0, tiled=True)
    projected = jnp.sum(shares.astype(F32), axis=0).astype(BF16)
    swap = []
    for z in range(Z):
        for i in range(YC):
            for g in range(HEADS):
                swap.append(((z * YC + i) * HEADS + g, (g * YC + i) * HEADS + z))
    return lax.ppermute(projected, ("seq", "head"), swap)


def solution(mesh):
    return jax.shard_map(
        body,
        mesh=mesh,
        in_specs=(
            P("seq", "head"),
            P("head", "seq", None),
            P("head", "seq", None),
            P("seq", "head"),
            P("seq", "head"),
            P("seq"),
            P(),
            P("head", "seq"),
        ),
        out_specs=P("head", "seq"),
        check_vma=False,
    )
```

time: 775 us -> 192 us (0.25)
  the two profiles are of different devices: /device:TPU:1 before, /device:TPU:225 now
where the time goes in v1:
time: 192 us; the launch traced here: 190 us
  waiting for transfers between devices  78.2 us (41%)
  blocking collectives  33.6 us (18%)
  starting transfers between devices  27.4 us (14%)
  Pallas kernels  23.1 us (12%)
  between operations  14.2 us (7%)
  local copies, waits for them, and re-layouts  8.81 us (5%)
  matrix products  3.44 us (2%)
    ppermute x13, waiting for transfers between devices, seq_permute(): return lax.ppermute(value, 'seq', pairs)  59.8 us
    ppermute x13, starting transfers between devices, seq_permute(): return lax.ppermute(value, 'seq', pairs)  24.2 us
    all_to_all x1, blocking collectives, body(): shares = lax.all_to_all(shares, 'head', 0, 0, tiled=True)  22.6 us
    pallas_call x1, Pallas kernels, attention(): pl.pallas_call(attention_kernel, out_shape=[jax.ShapeDtypeStruct((TOK, WI...  20.9 us
    ppermute x1, waiting for transfers between devices, body(): return lax.ppermute(projected, ('seq', 'head'), swap)  17.7 us
    all_gather x1, blocking collectives, body(): lax.all_gather(attended, 'seq', axis=0, tiled=True, axis_index_groups=pla...  11 us
    unnamed x25, local copies, waits for them, and re-layouts  4.79 us
  transfers between devices with their start and end apart: 15, of which 6 were waited for; matrix products, arithmetic and copies ran while one was open for 4% of the time, Pallas kernels for 12%

profile of v1, /device:TPU:225, one launch (start us, length us, event | category | flops | bytes accessed | tf_op | source)
XLA Modules:
  0.0 189.7 jit_solution(15948340226643611622)
XLA Ops:
  6.5 0.7 all-gather.3.cloned.1.call-update
  7.9 1.0 bitcast_dynamic-update-slice_fusion.1
  8.9 1.0 bitcast_dynamic-update-slice_fusion
  9.9 0.7 constant_dynamic-update-slice_fusion.2
  10.6 0.7 constant_dynamic-update-slice_fusion.1
  11.4 0.1 constant_dynamic-update-slice_fusion.refs_4_
  11.4 1.3 collective-permute-start.4
  12.8 0.7 collective-permute-start.6
  13.5 0.6 collective-permute-start.8
  14.1 1.5 collective-permute-start.3
  15.6 1.2 collective-permute-start
  16.8 0.8 reshape.20
  17.7 42.9 %collective-permute-done.refs_0_ = bf16[64,1024]{1,0:T(8,128)(2,1)S(1)} collective-permute-done((bf16[64,1024]{1,0:T(8,128)(2,1)}, bf16[64,1024]{1,0:T(8,128)(2,1)S(1)}, u32[]{:S(2)}, u32[]{:S(2)}) %collective-permute-start) | collective-permute-done | bytes 131104 | tf_op jit(solution)/shard_map/ppermute | solution.py:36
  60.6 0.0 collective-permute-start.1
  60.6 0.0 collective-permute-done.4.refs_6_
  60.6 6.1 %collective-permute-start.5 = (bf16[2192,128]{1,0:T(8,128)(2,1)S(1)}, bf16[2192,128]{1,0:T(8,128)(2,1)S(1)}, u32[]{:S(2)}, u32[]{:S(2)}) collective-permute-start(bf16[2192,128]{1,0:T(8,128)(2,1)S(1)} %collective-permute-done.4.refs_6_), channel_id=1, source_target_pairs={{0,8},{8,0},{16,24},{24,16},{32,40},{40,32},{48,56},{56,48},{64,72... | collective-permute-start | bytes 1683464 | tf_op jit(solution)/shard_map/ppermute | solution.py:36
  66.7 0.0 collective-permute-done.6.refs_8_
  66.7 0.1 collective-permute-start.7
  66.8 0.0 collective-permute-done.8.refs_10_
  66.8 0.4 collective-permute-start.9
  67.2 0.7 compare_select_fusion
  67.9 3.1 %collective-permute-done.1.refs_1_ = bf16[64,1024]{1,0:T(8,128)(2,1)} collective-permute-done((bf16[64,1024]{1,0:T(8,128)(2,1)}, bf16[64,1024]{1,0:T(8,128)(2,1)}, u32[]{:S(2)}, u32[]{:S(2)}) %collective-permute-start.1) | collective-permute-done | bytes 131104 | tf_op jit(solution)/shard_map/ppermute | solution.py:36
  71.0 2.7 %collective-permute-start.2 = (bf16[64,1024]{1,0:T(8,128)(2,1)}, bf16[64,1024]{1,0:T(8,128)(2,1)}, u32[]{:S(2)}, u32[]{:S(2)}) collective-permute-start(bf16[64,1024]{1,0:T(8,128)(2,1)} %refs_3_.1), channel_id=1, source_target_pairs={{0,64},{8,72},{16,80},{24,88},{32,96},{40,104},{48,112},{56,120},{... | collective-permute-start | bytes 393224 | tf_op jit(solution)/shard_map/ppermute | solution.py:36
  73.7 0.8 reshape.19
  74.4 0.1 broadcast_in_dim.28
  74.5 0.6 gather_fusion
  75.1 0.7 tile.10.refs_12_
  75.8 5.7 %collective-permute-done.2.refs_2_ = bf16[64,1024]{1,0:T(8,128)(2,1)} collective-permute-done((bf16[64,1024]{1,0:T(8,128)(2,1)}, bf16[64,1024]{1,0:T(8,128)(2,1)}, u32[]{:S(2)}, u32[]{:S(2)}) %collective-permute-start.2) | collective-permute-done | bytes 131104 | tf_op jit(solution)/shard_map/ppermute | solution.py:36
  81.5 0.0 collective-permute-done.3.refs_5_
  81.5 0.0 collective-permute-done.5.refs_7_
  81.5 0.0 collective-permute-done.9.refs_11_
  81.5 1.0 broadcast_in_dim.29.refs_13_
  82.6 0.0 copy-done.5
  82.6 20.9 %attention.1 = (bf16[64,1152]{1,0:T(8,128)(2,1)}, bf16[64,1152]{1,0:T(8,128)(2,1)}, bf16[64,1152]{1,0:T(8,128)(2,1)}, bf16[64,1152]{1,0:T(8,128)(2,1)}) custom-call(bf16[64,1024]{1,0:T(8,128)(2,1)} %copy-done.9, bf16[64,1024]{1,0:T(8,128)(2,1)} %collective-permute-done.1.refs_1_, bf16[64,1024]{1,0:T(8,128)(2,1)} %collective-permute-done.2.refs_2_, ...), custom_call_target="tpu_custom_call" | custom-call | tf_op jit(solution)/shard_map/attention/pallas_call | solution.py:160
  103.5 7.1 %collective-permute-start.10 = (bf16[64,1152]{1,0:T(8,128)(2,1)}, bf16[64,1152]{1,0:T(8,128)(2,1)S(1)}, u32[]{:S(2)}, u32[]{:S(2)}) collective-permute-start(bf16[64,1152]{1,0:T(8,128)(2,1)} %get-tuple-element.9), channel_id=1, source_target_pairs={{0,128},{8,136},{16,144},{24,152},{32,160},{40,168},{48,176},{56,1... | collective-permute-start | bytes 442376 | tf_op jit(solution)/shard_map/ppermute | solution.py:36
  110.6 0.3 collective-permute-start.11
  110.9 2.1 %collective-permute-start.12 = (bf16[64,1152]{1,0:T(8,128)(2,1)}, bf16[64,1152]{1,0:T(8,128)(2,1)S(1)}, u32[]{:S(2)}, u32[]{:S(2)}) collective-permute-start(bf16[64,1152]{1,0:T(8,128)(2,1)} %get-tuple-element.11), channel_id=1, source_target_pairs={{0,192},{8,200},{16,208},{24,216},{32,224},{40,232},{48,240},{56,2... | collective-permute-start | bytes 442376 | tf_op jit(solution)/shard_map/ppermute | solution.py:36
  113.0 3.7 %collective-permute-done.10.a_ref = bf16[64,1152]{1,0:T(8,128)(2,1)S(1)} collective-permute-done((bf16[64,1152]{1,0:T(8,128)(2,1)}, bf16[64,1152]{1,0:T(8,128)(2,1)S(1)}, u32[]{:S(2)}, u32[]{:S(2)}) %collective-permute-start.10) | collective-permute-done | bytes 147488 | tf_op jit(solution)/shard_map/ppermute | solution.py:36
  116.7 4.4 %collective-permute-done.12.c_ref = bf16[64,1152]{1,0:T(8,128)(2,1)S(1)} collective-permute-done((bf16[64,1152]{1,0:T(8,128)(2,1)}, bf16[64,1152]{1,0:T(8,128)(2,1)S(1)}, u32[]{:S(2)}, u32[]{:S(2)}) %collective-permute-start.12) | collective-permute-done | bytes 147488 | tf_op jit(solution)/shard_map/ppermute | solution.py:36
  121.1 0.7 copy-done.8
  121.8 2.3 %merge.1 = bf16[64,1024]{1,0:T(8,128)(2,1)} custom-call(bf16[64,1152]{1,0:T(8,128)(2,1)} %copy-done.6, bf16[64,1152]{1,0:T(8,128)(2,1)} %copy-done.7, bf16[64,1152]{1,0:T(8,128)(2,1)} %copy-done.8, bf16[64,1152]{1,0:T(8,128)(2,1)} %get-tuple-element.12.d_ref), custom_call_target="tpu_custom_call" | custom-call | tf_op jit(solution)/shard_map/merge/pallas_call | solution.py:196
  124.0 11.0 %all_gather.9 = bf16[256,1024]{1,0:T(8,128)(2,1)S(1)} all-gather(bf16[64,1024]{1,0:T(8,128)(2,1)} %merge.1), channel_id=1, replica_groups={{0,8,16,24},{32,40,48,56},{64,72,80,88},{96,104,112,120},{128,136,144,1..., dimensions={0}, use_global_device_ids=true | all-gather | bytes 655360 | tf_op jit(solution)/shard_map/all_gather | solution.py:243
  135.0 3.4 %fusion = bf16[8,256,256]{2,1,0:T(8,128)(2,1)S(1)} fusion(bf16[8,1024,256]{2,1,0:T(8,128)(2,1)} %bitcast.26, bf16[256,1024]{1,0:T(8,128)(2,1)S(1)} %all_gather.9), kind=kOutput, calls=%fused_computation.2 | convolution fusion | flops 1074266112 | bytes 5767168 | tf_op jit(solution)/shard_map/tf,zfc->ztc/dot_general | solution.py:244
  138.5 22.6 %all_to_all.5 = bf16[8,256,256]{2,1,0:T(8,128)(2,1)S(1)} all-to-all(bf16[8,256,256]{2,1,0:T(8,128)(2,1)S(1)} %fusion), channel_id=1, replica_groups=mesh['seq'=32,'head'=8] {'head'}, dimensions={0} | all-to-all | bytes 2097152 | tf_op jit(solution)/shard_map/all_to_all | solution.py:245
  161.1 0.1 reduce_sum.12
  161.3 3.3 %collective-permute-start.13 = (bf16[256,256]{1,0:T(8,128)(2,1)S(1)}, bf16[256,256]{1,0:T(8,128)(2,1)S(1)}, u32[]{:S(2)}, u32[]{:S(2)}) collective-permute-start(bf16[256,256]{1,0:T(8,128)(2,1)S(1)} %reduce_sum.12), channel_id=1, source_target_pairs={{0,0},{1,32},{2,64},{3,96},{4,128},{5,160},{6,192},{7,224},{8,8},{... | collective-permute-start | bytes 393224 | tf_op jit(solution)/shard_map/ppermute | solution.py:252
  164.5 17.7 %collective-permute-done.13 = bf16[256,256]{1,0:T(8,128)(2,1)S(1)} collective-permute-done((bf16[256,256]{1,0:T(8,128)(2,1)S(1)}, bf16[256,256]{1,0:T(8,128)(2,1)S(1)}, u32[]{:S(2)}, u32[]{:S(2)}) %collective-permute-start.13) | collective-permute-done | bytes 131104 | tf_op jit(solution)/shard_map/ppermute | solution.py:252
  182.2 0.7 copy.16
  (33 shorter events, 0.1 us)
Async XLA Ops:
  6.5 128.5 %all-gather.3.cloned.1.call-start = ((), (), s32[]{:S(2)}) async-start(), calls=%async_computation.1 | async-start | bytes 4718592 | tf_op jit(solution)/shard_map/all_gather | solution.py:242
  11.4 71.1 %copy-start = (bf16[2192,128]{1,0:T(8,128)(2,1)}, bf16[2192,128]{1,0:T(8,128)(2,1)S(1)}, u32[]{:S(2)}) copy-start(bf16[2192,128]{1,0:T(8,128)(2,1)S(1)} %constant_dynamic-update-slice_fusion.refs_4_) | copy-start | bytes 1683460
  11.4 49.1 %collective-permute-start.4 = (bf16[2192,128]{1,0:T(8,128)(2,1)S(1)}, bf16[2192,128]{1,0:T(8,128)(2,1)S(1)}, u32[]{:S(2)}, u32[]{:S(2)}) collective-permute-start(bf16[2192,128]{1,0:T(8,128)(2,1)S(1)} %constant_dynamic-update-slice_fusion.refs_4_), channel_id=1, source_target_pairs={{0,16},{8,24},{16,0},{24,8},{32,48},{40,56},{48,32},{56,40},{64,80... | collective-permute-start | bytes 1683464 | tf_op jit(solution)/shard_map/ppermute | solution.py:36
  12.8 53.9 %collective-permute-start.6 = (bf16[2192,128]{1,0:T(8,128)(2,1)S(1)}, bf16[2192,128]{1,0:T(8,128)(2,1)S(1)}, u32[]{:S(2)}, u32[]{:S(2)}) collective-permute-start(bf16[2192,128]{1,0:T(8,128)(2,1)S(1)} %constant_dynamic-update-slice_fusion.refs_4_), channel_id=1, source_target_pairs={{0,32},{8,40},{16,48},{24,56},{32,0},{40,8},{48,16},{56,24},{64,96... | collective-permute-start | bytes 1683464 | tf_op jit(solution)/shard_map/ppermute | solution.py:36
  13.5 53.3 %collective-permute-start.8 = (bf16[2192,128]{1,0:T(8,128)(2,1)S(1)}, bf16[2192,128]{1,0:T(8,128)(2,1)S(1)}, u32[]{:S(2)}, u32[]{:S(2)}) collective-permute-start(bf16[2192,128]{1,0:T(8,128)(2,1)S(1)} %constant_dynamic-update-slice_fusion.refs_4_), channel_id=1, source_target_pairs={{0,48},{8,56},{16,32},{24,40},{32,16},{40,24},{48,0},{56,8},{64,11... | collective-permute-start | bytes 1683464 | tf_op jit(solution)/shard_map/ppermute | solution.py:36
  14.1 67.4 %collective-permute-start.3 = (bf16[2192,128]{1,0:T(8,128)(2,1)S(1)}, bf16[2192,128]{1,0:T(8,128)(2,1)S(1)}, u32[]{:S(2)}, u32[]{:S(2)}) collective-permute-start(bf16[2192,128]{1,0:T(8,128)(2,1)S(1)} %constant_dynamic-update-slice_fusion.refs_4_), channel_id=1, source_target_pairs={{0,8},{8,0},{16,24},{24,16},{32,40},{40,32},{48,56},{56,48},{64,72... | collective-permute-start | bytes 1683464 | tf_op jit(solution)/shard_map/ppermute | solution.py:36
  15.6 44.9 %collective-permute-start = (bf16[64,1024]{1,0:T(8,128)(2,1)}, bf16[64,1024]{1,0:T(8,128)(2,1)S(1)}, u32[]{:S(2)}, u32[]{:S(2)}) collective-permute-start(bf16[64,1024]{1,0:T(8,128)(2,1)} %refs_3_.1), channel_id=1, source_target_pairs={{0,128},{8,136},{16,144},{24,152},{32,160},{40,168},{48,176},{56,1... | collective-permute-start | bytes 393224 | tf_op jit(solution)/shard_map/ppermute | solution.py:36
  60.6 22.0 %copy-start.9 = (bf16[64,1024]{1,0:T(8,128)(2,1)}, bf16[64,1024]{1,0:T(8,128)(2,1)S(1)}, u32[]{:S(2)}) copy-start(bf16[64,1024]{1,0:T(8,128)(2,1)S(1)} %collective-permute-done.refs_0_) | copy-start | bytes 393220
  60.6 10.4 %collective-permute-start.1 = (bf16[64,1024]{1,0:T(8,128)(2,1)}, bf16[64,1024]{1,0:T(8,128)(2,1)}, u32[]{:S(2)}, u32[]{:S(2)}) collective-permute-start(bf16[64,1024]{1,0:T(8,128)(2,1)} %refs_3_.1), channel_id=1, source_target_pairs={{0,192},{8,200},{16,208},{24,216},{32,224},{40,232},{48,240},{56,2... | collective-permute-start | bytes 393224 | tf_op jit(solution)/shard_map/ppermute | solution.py:36
  60.6 22.0 %copy-start.1 = (bf16[2192,128]{1,0:T(8,128)(2,1)}, bf16[2192,128]{1,0:T(8,128)(2,1)S(1)}, u32[]{:S(2)}) copy-start(bf16[2192,128]{1,0:T(8,128)(2,1)S(1)} %collective-permute-done.4.refs_6_) | copy-start | bytes 1683460
  60.6 20.9 %collective-permute-start.5 = (bf16[2192,128]{1,0:T(8,128)(2,1)S(1)}, bf16[2192,128]{1,0:T(8,128)(2,1)S(1)}, u32[]{:S(2)}, u32[]{:S(2)}) collective-permute-start(bf16[2192,128]{1,0:T(8,128)(2,1)S(1)} %collective-permute-done.4.refs_6_), channel_id=1, source_target_pairs={{0,8},{8,0},{16,24},{24,16},{32,40},{40,32},{48,56},{56,48},{64,72... | collective-permute-start | bytes 1683464 | tf_op jit(solution)/shard_map/ppermute | solution.py:36
  66.7 15.9 %copy-start.2 = (bf16[2192,128]{1,0:T(8,128)(2,1)}, bf16[2192,128]{1,0:T(8,128)(2,1)S(1)}, u32[]{:S(2)}) copy-start(bf16[2192,128]{1,0:T(8,128)(2,1)S(1)} %collective-permute-done.6.refs_8_) | copy-start | bytes 1683460
  66.7 14.8 %collective-permute-start.7 = (bf16[2192,128]{1,0:T(8,128)(2,1)S(1)}, bf16[2192,128]{1,0:T(8,128)(2,1)}, u32[]{:S(2)}, u32[]{:S(2)}) collective-permute-start(bf16[2192,128]{1,0:T(8,128)(2,1)S(1)} %collective-permute-done.6.refs_8_), channel_id=1, source_target_pairs={{0,8},{8,0},{16,24},{24,16},{32,40},{40,32},{48,56},{56,48},{64,72... | collective-permute-start | bytes 1683464 | tf_op jit(solution)/shard_map/ppermute | solution.py:36
  66.8 15.8 %copy-start.3 = (bf16[2192,128]{1,0:T(8,128)(2,1)}, bf16[2192,128]{1,0:T(8,128)(2,1)S(1)}, u32[]{:S(2)}) copy-start(bf16[2192,128]{1,0:T(8,128)(2,1)S(1)} %collective-permute-done.8.refs_10_) | copy-start | bytes 1683460
  66.8 14.7 %collective-permute-start.9 = (bf16[2192,128]{1,0:T(8,128)(2,1)S(1)}, bf16[2192,128]{1,0:T(8,128)(2,1)}, u32[]{:S(2)}, u32[]{:S(2)}) collective-permute-start(bf16[2192,128]{1,0:T(8,128)(2,1)S(1)} %collective-permute-done.8.refs_10_), channel_id=1, source_target_pairs={{0,8},{8,0},{16,24},{24,16},{32,40},{40,32},{48,56},{56,48},{64,72... | collective-permute-start | bytes 1683464 | tf_op jit(solution)/shard_map/ppermute | solution.py:36
  71.0 10.5 %collective-permute-start.2 = (bf16[64,1024]{1,0:T(8,128)(2,1)}, bf16[64,1024]{1,0:T(8,128)(2,1)}, u32[]{:S(2)}, u32[]{:S(2)}) collective-permute-start(bf16[64,1024]{1,0:T(8,128)(2,1)} %refs_3_.1), channel_id=1, source_target_pairs={{0,64},{8,72},{16,80},{24,88},{32,96},{40,104},{48,112},{56,120},{... | collective-permute-start | bytes 393224 | tf_op jit(solution)/shard_map/ppermute | solution.py:36
  81.5 1.1 copy-start.4
  81.5 1.1 copy-start.5
  103.5 13.2 %collective-permute-start.10 = (bf16[64,1152]{1,0:T(8,128)(2,1)}, bf16[64,1152]{1,0:T(8,128)(2,1)S(1)}, u32[]{:S(2)}, u32[]{:S(2)}) collective-permute-start(bf16[64,1152]{1,0:T(8,128)(2,1)} %get-tuple-element.9), channel_id=1, source_target_pairs={{0,128},{8,136},{16,144},{24,152},{32,160},{40,168},{48,176},{56,1... | collective-permute-start | bytes 442376 | tf_op jit(solution)/shard_map/ppermute | solution.py:36
  110.6 6.1 %collective-permute-start.11 = (bf16[64,1152]{1,0:T(8,128)(2,1)}, bf16[64,1152]{1,0:T(8,128)(2,1)S(1)}, u32[]{:S(2)}, u32[]{:S(2)}) collective-permute-start(bf16[64,1152]{1,0:T(8,128)(2,1)} %get-tuple-element.10), channel_id=1, source_target_pairs={{0,64},{8,72},{16,80},{24,88},{32,96},{40,104},{48,112},{56,120},{... | collective-permute-start | bytes 442376 | tf_op jit(solution)/shard_map/ppermute | solution.py:36
  110.9 10.2 %collective-permute-start.12 = (bf16[64,1152]{1,0:T(8,128)(2,1)}, bf16[64,1152]{1,0:T(8,128)(2,1)S(1)}, u32[]{:S(2)}, u32[]{:S(2)}) collective-permute-start(bf16[64,1152]{1,0:T(8,128)(2,1)} %get-tuple-element.11), channel_id=1, source_target_pairs={{0,192},{8,200},{16,208},{24,216},{32,224},{40,232},{48,240},{56,2... | collective-permute-start | bytes 442376 | tf_op jit(solution)/shard_map/ppermute | solution.py:36
  116.7 4.4 %copy-start.6 = (bf16[64,1152]{1,0:T(8,128)(2,1)}, bf16[64,1152]{1,0:T(8,128)(2,1)S(1)}, u32[]{:S(2)}) copy-start(bf16[64,1152]{1,0:T(8,128)(2,1)S(1)} %collective-permute-done.10.a_ref) | copy-start | bytes 442372
  116.7 4.4 %copy-start.7 = (bf16[64,1152]{1,0:T(8,128)(2,1)}, bf16[64,1152]{1,0:T(8,128)(2,1)S(1)}, u32[]{:S(2)}) copy-start(bf16[64,1152]{1,0:T(8,128)(2,1)S(1)} %collective-permute-done.11.b_ref) | copy-start | bytes 442372
  121.1 0.7 copy-start.8
  161.3 20.9 %collective-permute-start.13 = (bf16[256,256]{1,0:T(8,128)(2,1)S(1)}, bf16[256,256]{1,0:T(8,128)(2,1)S(1)}, u32[]{:S(2)}, u32[]{:S(2)}) collective-permute-start(bf16[256,256]{1,0:T(8,128)(2,1)S(1)} %reduce_sum.12), channel_id=1, source_target_pairs={{0,0},{1,32},{2,64},{3,96},{4,128},{5,160},{6,192},{7,224},{8,8},{... | collective-permute-start | bytes 393224 | tf_op jit(solution)/shard_map/ppermute | solution.py:252
Sparse Core Ops, SparseCore 0:
  9.1 81.5 all-gather.2
